TPU v7x, 32 devices: a whole 2x2x4 slice. The times are simulated.
32 devices in a mesh: dp: 16 (over z, y, x), tensor: 2 (over core).
Axes of the slice: x: 2, y: 2, z: 4, core: 2. Of those that a mesh axis runs over, the one named last changes fastest.
Arguments:
- hidden_in: bfloat16 [32768, 768], P(('dp', 'tensor')), may hold values from -6 to 6
- out_grad: bfloat16 [32768, 768], P(('dp', 'tensor')), may hold values from -6 to 6
- seq_lengths: int32 [16, 8], P('dp'), may hold values from 1 to 1024, as said below
- attn_gain: bfloat16 [768], P('dp'), may hold values from 0.099609375 to 1.8984375
- attn_shift: bfloat16 [768], P('dp'), may hold values from -1.75 to 1.75
- mlp_gain: bfloat16 [768], P('dp'), may hold values from 0.099609375 to 1.8984375
- mlp_shift: bfloat16 [768], P('dp'), may hold values from -1.75 to 1.75
- qkv_weight: bfloat16 [768, 12, 192], P('dp', 'tensor'), may hold values from -0.21875 to 0.21875
- qkv_bias: bfloat16 [2304], P('dp'), may hold values from -1.75 to 1.75
- dense_weight: bfloat16 [768, 12, 64], P('dp', 'tensor'), may hold values from -0.875 to 0.875
- dense_bias: bfloat16 [768], P('dp'), may hold values from -1.75 to 1.75
- fc_weight: bfloat16 [768, 3072], P('dp', 'tensor'), may hold values from -0.21875 to 0.21875
- fc_bias: bfloat16 [3072], P('dp'), may hold values from -1.75 to 1.75
- proj_weight: bfloat16 [768, 3072], P('dp', 'tensor'), may hold values from -0.15625 to 0.15625
- proj_bias: bfloat16 [768], P('dp'), may hold values from -1.75 to 1.75
Outputs:
- block_out: bfloat16 [32768, 768], P(('dp', 'tensor'))
- input_grad: float32 [32768, 768], P(('dp', 'tensor'))
- attn_gain_grad: float32 [768], P(('dp', 'tensor'))
- attn_shift_grad: float32 [768], P(('dp', 'tensor'))
- mlp_gain_grad: float32 [768], P(('dp', 'tensor'))
- mlp_shift_grad: float32 [768], P(('dp', 'tensor'))
- qkv_weight_grad: float32 [768, 12, 192], P('dp', 'tensor')
- qkv_bias_grad: float32 [2304], P(('dp', 'tensor'))
- dense_weight_grad: float32 [768, 12, 64], P('dp', 'tensor')
- dense_bias_grad: float32 [768], P(('dp', 'tensor'))
- fc_weight_grad: float32 [768, 3072], P('dp', 'tensor')
- fc_bias_grad: float32 [3072], P(('dp', 'tensor'))
- proj_weight_grad: float32 [768, 3072], P('dp', 'tensor')
- proj_bias_grad: float32 [768], P(('dp', 'tensor'))
Inputs may be any that keep to these rules, and one draw needn't show every extreme that they name: `seq_lengths`: row g lists the 8 sequences of group g in order; they are all 1 or longer and sum to 2048. One sequence of each row has exactly 1024 rows and covers rows 1023 and 1024 of its group.
All inputs are finite; a program needn't handle non-finite values.
Results may differ from a plain program's by a relative error of at most 0.012.
Values may be sent and summed in bfloat16 or wider, within the bound.
A program may use at most 256 MiB of HBM per device.

v0:
```python
import jax
import jax.numpy as jnp
from jax import lax
from jax.sharding import PartitionSpec as P


def layout(lengths, group_rows):
    seq_ends = jnp.cumsum(lengths)
    starts = seq_ends - lengths
    row_index = jnp.arange(group_rows, dtype=jnp.int32)
    seg_ids = jnp.sum((row_index[:, None] >= seq_ends[None, :]).astype(jnp.int32), axis=1)
    owner_mask = seg_ids[:, None] == jnp.arange(lengths.shape[0], dtype=jnp.int32)[None, :]
    positions = row_index - jnp.sum(jnp.where(owner_mask, starts[None, :], 0), axis=1)
    return (seg_ids, positions)


def layer_norm(values, gain_vec, shift_vec):
    average = jnp.mean(values, axis=-1, keepdims=True)
    centred = values - average
    spread = jnp.mean(centred * centred, axis=-1, keepdims=True)
    return centred * lax.rsqrt(spread + 1e-05) * gain_vec + shift_vec


def rotary_tables(positions, head_dim):
    rot_dims = head_dim // 4
    half_rot = rot_dims // 2
    inv_freq = 10000.0 ** (-(jnp.arange(half_rot, dtype=jnp.float32) * 2.0 / rot_dims))
    angles = positions.astype(jnp.float32)[:, None] * inv_freq[None, :]
    angles = jnp.concatenate([angles, angles], axis=-1)
    return (jnp.cos(angles), jnp.sin(angles))


def rotate(vectors, cosine_table, sine_table):
    rot_dims = cosine_table.shape[-1]
    half_rot = rot_dims // 2
    rot_part = vectors[..., :rot_dims]
    turned = jnp.concatenate([-rot_part[..., half_rot:], rot_part[..., :half_rot]], axis=-1)
    result = rot_part * cosine_table[:, None, :] + turned * sine_table[:, None, :]
    return jnp.concatenate([result, vectors[..., rot_dims:]], axis=-1)


def exact_gelu(values):
    return jax.nn.gelu(values, approximate=False)


def body(
    hidden_in,
    out_grad,
    seq_lengths,
    attn_gain,
    attn_shift,
    mlp_gain,
    mlp_shift,
    qkv_weight,
    qkv_bias,
    dense_weight,
    dense_bias,
    fc_weight,
    fc_bias,
    proj_weight,
    proj_bias,
):
    tensor_index = lax.axis_index("tensor")
    tensor_count = lax.axis_size("tensor")
    local_rows = hidden_in.shape[0]
    group_rows = local_rows * tensor_count
    gathered = (
        lax.all_gather(qkv_weight, "dp", axis=0, tiled=True),
        lax.all_gather(dense_weight, "dp", axis=0, tiled=True),
        lax.all_gather(fc_weight, "dp", axis=0, tiled=True),
        lax.all_gather(proj_weight, "dp", axis=0, tiled=True),
        lax.all_gather(attn_gain, "dp", axis=0, tiled=True),
        lax.all_gather(attn_shift, "dp", axis=0, tiled=True),
        lax.all_gather(mlp_gain, "dp", axis=0, tiled=True),
        lax.all_gather(mlp_shift, "dp", axis=0, tiled=True),
        lax.all_gather(qkv_bias, "dp", axis=0, tiled=True),
        lax.all_gather(dense_bias, "dp", axis=0, tiled=True),
        lax.all_gather(fc_bias, "dp", axis=0, tiled=True),
        lax.all_gather(proj_bias, "dp", axis=0, tiled=True),
    )
    (
        w_qkv,
        w_dense,
        w_fc,
        w_proj,
        gain_attn,
        shift_attn,
        gain_mlp,
        shift_mlp,
        bias_qkv,
        bias_dense,
        bias_fc,
        bias_proj,
    ) = gathered
    model_width = w_qkv.shape[0]
    head_count = w_qkv.shape[1]
    triple_width = w_qkv.shape[2]
    head_dim = w_dense.shape[2]
    hidden_units = w_fc.shape[1]
    qkv_cols = head_count * triple_width
    attn_cols = head_count * head_dim
    my_bias_qkv = lax.dynamic_slice_in_dim(bias_qkv, tensor_index * qkv_cols, qkv_cols).astype(
        jnp.float32
    )
    my_bias_fc = lax.dynamic_slice_in_dim(
        bias_fc, tensor_index * hidden_units, hidden_units
    ).astype(jnp.float32)
    gain_attn_f = gain_attn.astype(jnp.float32)
    shift_attn_f = shift_attn.astype(jnp.float32)
    gain_mlp_f = gain_mlp.astype(jnp.float32)
    shift_mlp_f = shift_mlp.astype(jnp.float32)
    seg_ids, positions = layout(seq_lengths[0], group_rows)
    x_rows = hidden_in.astype(jnp.float32)

    def norms(values, gain_one, shift_one, gain_two, shift_two):
        return (layer_norm(values, gain_one, shift_one), layer_norm(values, gain_two, shift_two))

    (normed_one, normed_two), norm_back = jax.vjp(
        norms, x_rows, gain_attn_f, shift_attn_f, gain_mlp_f, shift_mlp_f
    )
    normed_attn, normed_mlp = (
        lax.all_gather(normed_one.astype(jnp.bfloat16), "tensor", axis=0, tiled=True),
        lax.all_gather(normed_two.astype(jnp.bfloat16), "tensor", axis=0, tiled=True),
    )
    merged_lin = (
        jnp.dot(
            normed_attn, w_qkv.reshape(model_width, qkv_cols), preferred_element_type=jnp.float32
        )
        + my_bias_qkv
    )
    merged_lin = merged_lin.reshape(group_rows, head_count, triple_width)
    cosine_table, sine_table = rotary_tables(positions, head_dim)

    def turn_pair(query_lin, key_lin):
        return (
            rotate(query_lin, cosine_table, sine_table),
            rotate(key_lin, cosine_table, sine_table),
        )

    (query_rot, key_rot), turn_back = jax.vjp(
        turn_pair, merged_lin[..., :head_dim], merged_lin[..., head_dim : 2 * head_dim]
    )
    query_low = query_rot.astype(jnp.bfloat16)
    key_low = key_rot.astype(jnp.bfloat16)
    value_low = merged_lin[..., 2 * head_dim :].astype(jnp.bfloat16)
    score_scale = head_dim ** (-0.5)
    block_rows = min(512, group_rows)
    block_count = group_rows // block_rows
    row_index = jnp.arange(group_rows, dtype=jnp.int32)

    def masked_scores(number):
        begin_row = number * block_rows
        end_row = begin_row + block_rows
        scores = (
            jnp.einsum(
                "qhd,khd->hqk",
                query_low[begin_row:end_row],
                key_low[:end_row],
                preferred_element_type=jnp.float32,
            )
            * score_scale
        )
        allowed = (row_index[None, :end_row] <= row_index[begin_row:end_row, None]) & (
            seg_ids[None, :end_row] == seg_ids[begin_row:end_row, None]
        )
        return jnp.where(allowed[None], scores, -1e30)

    head_blocks = []
    log_totals = []
    for number in range(block_count):
        end_row = (number + 1) * block_rows
        scores = masked_scores(number)
        peak_score = jnp.max(scores, axis=-1, keepdims=True)
        weights = jnp.exp(scores - peak_score)
        norm_total = jnp.sum(weights, axis=-1, keepdims=True)
        log_totals.append(peak_score + jnp.log(norm_total))
        prob_low = (weights / norm_total).astype(jnp.bfloat16)
        head_blocks.append(
            jnp.einsum(
                "hqk,khd->qhd", prob_low, value_low[:end_row], preferred_element_type=jnp.float32
            )
        )
    heads_flat = (
        jnp.concatenate(head_blocks, axis=0).astype(jnp.bfloat16).reshape(group_rows, attn_cols)
    )
    attn_part = jnp.einsum(
        "gc,dc->gd",
        heads_flat,
        w_dense.reshape(model_width, attn_cols),
        preferred_element_type=jnp.float32,
    )
    fc_pre = jnp.dot(normed_mlp, w_fc, preferred_element_type=jnp.float32) + my_bias_fc
    act_full, gelu_back = jax.vjp(exact_gelu, fc_pre)
    act_low = act_full.astype(jnp.bfloat16)
    mlp_part = jnp.einsum("gf,df->gd", act_low, w_proj, preferred_element_type=jnp.float32)
    branch_rows = lax.psum_scatter(
        (attn_part + mlp_part).astype(jnp.bfloat16), "tensor", scatter_dimension=0, tiled=True
    ).astype(jnp.float32)
    block_out = (
        x_rows + branch_rows + bias_dense.astype(jnp.float32) + bias_proj.astype(jnp.float32)
    ).astype(jnp.bfloat16)
    w_qkv, w_dense, w_fc, w_proj = (
        lax.all_gather(qkv_weight, "dp", axis=0, tiled=True),
        lax.all_gather(dense_weight, "dp", axis=0, tiled=True),
        lax.all_gather(fc_weight, "dp", axis=0, tiled=True),
        lax.all_gather(proj_weight, "dp", axis=0, tiled=True),
    )
    cot_all = lax.all_gather(out_grad, "tensor", axis=0, tiled=True)
    grad_act = jnp.dot(cot_all, w_proj, preferred_element_type=jnp.float32)
    grad_proj = jnp.einsum("gd,gf->df", cot_all, act_low, preferred_element_type=jnp.float32)
    grad_pre = gelu_back(grad_act)[0].astype(jnp.bfloat16)
    grad_fc = jnp.einsum("gd,gf->df", normed_mlp, grad_pre, preferred_element_type=jnp.float32)
    fc_bias_part = jnp.sum(grad_pre, axis=0, dtype=jnp.float32)
    grad_normed_mlp = jnp.einsum("gf,df->gd", grad_pre, w_fc, preferred_element_type=jnp.float32)
    dense_flat = w_dense.reshape(model_width, attn_cols)
    grad_heads = (
        jnp.dot(cot_all, dense_flat, preferred_element_type=jnp.float32)
        .astype(jnp.bfloat16)
        .reshape(group_rows, head_count, head_dim)
    )
    grad_dense = jnp.einsum(
        "gd,gc->dc", cot_all, heads_flat, preferred_element_type=jnp.float32
    ).reshape(model_width, head_count, head_dim)
    query_grads = []
    grad_key = jnp.zeros((group_rows, head_count, head_dim), jnp.float32)
    grad_value = jnp.zeros((group_rows, head_count, head_dim), jnp.float32)
    for number in range(block_count):
        begin_row = number * block_rows
        end_row = begin_row + block_rows
        probs = jnp.exp(masked_scores(number) - log_totals[number])
        heads_blk = grad_heads[begin_row:end_row]
        grad_probs = jnp.einsum(
            "qhd,khd->hqk", heads_blk, value_low[:end_row], preferred_element_type=jnp.float32
        )
        row_delta = jnp.sum(probs * grad_probs, axis=-1, keepdims=True)
        grad_scores = (probs * (grad_probs - row_delta)).astype(jnp.bfloat16)
        query_grads.append(
            jnp.einsum(
                "hqk,khd->qhd", grad_scores, key_low[:end_row], preferred_element_type=jnp.float32
            )
            * score_scale
        )
        grad_key = grad_key.at[:end_row].add(
            jnp.einsum(
                "hqk,qhd->khd",
                grad_scores,
                query_low[begin_row:end_row],
                preferred_element_type=jnp.float32,
            )
            * score_scale
        )
        grad_value = grad_value.at[:end_row].add(
            jnp.einsum(
                "hqk,qhd->khd",
                probs.astype(jnp.bfloat16),
                heads_blk,
                preferred_element_type=jnp.float32,
            )
        )
    grad_query = jnp.concatenate(query_grads, axis=0)
    grad_query_lin, grad_key_lin = turn_back((grad_query, grad_key))
    grad_merged = (
        jnp.concatenate([grad_query_lin, grad_key_lin, grad_value], axis=-1)
        .astype(jnp.bfloat16)
        .reshape(group_rows, qkv_cols)
    )
    grad_qkv = jnp.einsum(
        "gd,gc->dc", normed_attn, grad_merged, preferred_element_type=jnp.float32
    ).reshape(model_width, head_count, triple_width)
    qkv_bias_part = jnp.sum(grad_merged, axis=0, dtype=jnp.float32)
    grad_normed_attn = jnp.einsum(
        "gc,dc->gd",
        grad_merged,
        w_qkv.reshape(model_width, qkv_cols),
        preferred_element_type=jnp.float32,
    )
    cot_rows = out_grad.astype(jnp.float32)
    local_attn, local_mlp = (
        lax.psum_scatter(
            grad_normed_attn.astype(jnp.bfloat16), "tensor", scatter_dimension=0, tiled=True
        ).astype(jnp.float32),
        lax.psum_scatter(
            grad_normed_mlp.astype(jnp.bfloat16), "tensor", scatter_dimension=0, tiled=True
        ).astype(jnp.float32),
    )
    grad_x, grad_gain_attn, grad_shift_attn, grad_gain_mlp, grad_shift_mlp = norm_back(
        (local_attn, local_mlp)
    )
    input_grad = cot_rows + grad_x
    cot_sums = jnp.sum(cot_rows, axis=0)
    full_qkv_bias = lax.dynamic_update_slice_in_dim(
        jnp.zeros((qkv_cols * tensor_count,), jnp.float32),
        qkv_bias_part,
        tensor_index * qkv_cols,
        0,
    )
    full_fc_bias = lax.dynamic_update_slice_in_dim(
        jnp.zeros((hidden_units * tensor_count,), jnp.float32),
        fc_bias_part,
        tensor_index * hidden_units,
        0,
    )
    small_sums = (
        lax.psum_scatter(grad_gain_attn, ("dp", "tensor"), scatter_dimension=0, tiled=True),
        lax.psum_scatter(grad_shift_attn, ("dp", "tensor"), scatter_dimension=0, tiled=True),
        lax.psum_scatter(grad_gain_mlp, ("dp", "tensor"), scatter_dimension=0, tiled=True),
        lax.psum_scatter(grad_shift_mlp, ("dp", "tensor"), scatter_dimension=0, tiled=True),
        lax.psum_scatter(full_qkv_bias, ("dp", "tensor"), scatter_dimension=0, tiled=True),
        lax.psum_scatter(cot_sums, ("dp", "tensor"), scatter_dimension=0, tiled=True),
        lax.psum_scatter(full_fc_bias, ("dp", "tensor"), scatter_dimension=0, tiled=True),
    )
    large_sums = (
        lax.psum_scatter(grad_qkv, "dp", scatter_dimension=0, tiled=True),
        lax.psum_scatter(grad_dense, "dp", scatter_dimension=0, tiled=True),
        lax.psum_scatter(grad_fc, "dp", scatter_dimension=0, tiled=True),
        lax.psum_scatter(grad_proj, "dp", scatter_dimension=0, tiled=True),
    )
    return (
        block_out,
        input_grad,
        small_sums[0],
        small_sums[1],
        small_sums[2],
        small_sums[3],
        large_sums[0],
        small_sums[4],
        large_sums[1],
        small_sums[5],
        large_sums[2],
        small_sums[6],
        large_sums[3],
        small_sums[5],
    )


def solution(mesh):
    in_specs = (
        P(("dp", "tensor"), None),
        P(("dp", "tensor"), None),
        P("dp", None),
        P("dp"),
        P("dp"),
        P("dp"),
        P("dp"),
        P("dp", "tensor", None),
        P("dp"),
        P("dp", "tensor", None),
        P("dp"),
        P("dp", "tensor"),
        P("dp"),
        P("dp", "tensor"),
        P("dp"),
    )
    out_specs = (
        P(("dp", "tensor"), None),
        P(("dp", "tensor"), None),
        P(("dp", "tensor")),
        P(("dp", "tensor")),
        P(("dp", "tensor")),
        P(("dp", "tensor")),
        P("dp", "tensor", None),
        P(("dp", "tensor")),
        P("dp", "tensor", None),
        P(("dp", "tensor")),
        P("dp", "tensor"),
        P(("dp", "tensor")),
        P("dp", "tensor"),
        P(("dp", "tensor")),
    )
    return jax.shard_map(body, mesh=mesh, in_specs=in_specs, out_specs=out_specs, check_vma=False)
```

profile of v0, /device:TPU:0, one launch (start us, length us, event | category | flops | bytes accessed | tf_op | source)
XLA Modules:
  0.0 1064.3 jit_solution(6079659336549797893)
XLA Ops:
  18.7 79.0 %all-reduce.26 = (bf16[768]{0:T(1024)(128)(2,1)S(1)}, bf16[768]{0:T(1024)(128)(2,1)S(1)}, bf16[3072]{0:T(1024)(128)(2,1)S(1)}, bf16[768]{0:T(1024)(128)(2,1)S(1)...) all-reduce(bf16[768]{0:T(1024)(128)(2,1)S(1)} %dynamic-update-slice, ...), channel_id=1, replica_groups=mesh['dp'=16,'tensor'=2] {'dp'}, use_global_device_ids=true, to_apply=%add.14 | all-reduce | flops 9984 | bytes 39936
  105.9 44.1 %all_gather.54 = bf16[768,6,64]{2,0,1:T(8,128)(2,1)S(1)} all-gather(bf16[48,6,64]{2,0,1:T(8,128)(2,1)S(1)} %copy-done.50), channel_id=1, replica_groups=mesh['dp'=16,'tensor'=2] {'dp'}, dimensions={0}, use_global_device_ids=true | all-gather | bytes 626688 | tf_op jit(solution)/shard_map/all_gather | solution.py:69
  157.1 3.3 convolution_convert_fusion.1
  161.7 3.3 copy.54
  165.0 5.8 convolution_add_fusion
  178.1 4.0 multiply_reduce_fusion.3
  182.0 4.6 multiply_convert_fusion.4
  194.6 6.1 multiply_reduce_fusion.2
  200.7 6.3 multiply_convert_fusion.2
  211.7 8.4 fusion.153
  220.1 9.0 fusion.2
  229.1 12.9 %multiply_reduce_fusion.1 = (f32[6,512]{1,0:T(8,128)S(1)}, f32[6,512,1536]{2,1,0:T(8,128)}) fusion(f32[6,512,1536]{2,1,0:T(8,128)} %get-tuple-element.251, f32[6,512]{1,0:T(8,128)S(1)} %log_add_fusion.1, bf16[512,6,64]{0,2,1:T(8,128)(2,1)} %bitcast.138, bf16[2048,6,192]{0,2,1:T(8,128)(2,1)} %copy-done.9), kind=kOutput, calls=%fused_computation.10 | convolution fusion | flops 618132480 | bytes 39346176 | tf_op jit(solution)/shard_map/qhd,khd->hqk/dot_general | solution.py:232
  242.1 13.0 %multiply_convert_fusion.1 = bf16[6,512,1536]{2,1,0:T(8,128)(2,1)S(1)} fusion(f32[6,512,1536]{2,1,0:T(8,128)} %get-tuple-element.257, f32[6,512,1536]{2,1,0:T(8,128)} %get-tuple-element.251, f32[6,512]{1,0:T(8,128)S(1)} %get-tuple-element.256, f32[6,512]{1,0:T(8,128)S(1)} %log_add_fusion.1), kind=kLoop, calls=%fused_computation.9 | loop fusion | flops 18874368 | bytes 47210496 | tf_op jit(solution)/shard_map/convert_element_type | solution.py:236
  255.1 3.8 fusion.100
  260.8 10.7 %fusion.154 = (f32[6,512]{1,0:T(8,128)S(1)}, f32[6,512,2048]{2,1,0:T(8,128)}) fusion(bf16[512,6,64]{0,2,1:T(8,128)(2,1)S(1)} %copy-done.32, bf16[2048,6,16]{0,2,1:T(8,128)(2,1)S(1)} %get-tuple-element.213, bf16[2048,6,48]{0,2,1:T(8,128)(2,1)S(1)} %get-tuple-element.219, pred[512,2048]{1,0:T(8,128)(4,1)S(1)} %copy-done.38), kind=kOutput, calls=%fused_computation.253 | convolution fusion | flops 827323392 | bytes 28192768 | tf_op jit(solution)/shard_map/qhd,khd->hqk/dot_general | solution.py:155
  271.5 10.5 fusion
  282.0 16.2 %multiply_reduce_fusion = (f32[6,512]{1,0:T(8,128)S(1)}, f32[6,512,2048]{2,1,0:T(8,128)}) fusion(f32[6,512,2048]{2,1,0:T(8,128)} %get-tuple-element.253, f32[6,512]{1,0:T(8,128)S(1)} %log_add_fusion, bf16[512,6,64]{0,2,1:T(8,128)(2,1)S(1)} %bitcast.136, bf16[2048,6,192]{0,2,1:T(8,128)(2,1)} %copy-done.9), kind=kOutput, calls=%fused_computation.1 | convolution fusion | flops 824177664 | bytes 52322304 | tf_op jit(solution)/shard_map/qhd,khd->hqk/dot_general | solution.py:232
  298.2 17.0 %multiply_convert_fusion = bf16[6,512,2048]{2,1,0:T(8,128)(2,1)S(1)} fusion(f32[6,512,2048]{2,1,0:T(8,128)} %get-tuple-element.255, f32[6,512,2048]{2,1,0:T(8,128)} %get-tuple-element.253, f32[6,512]{1,0:T(8,128)S(1)} %get-tuple-element.254, f32[6,512]{1,0:T(8,128)S(1)} %log_add_fusion), kind=kLoop, calls=%fused_computation | loop fusion | flops 25165824 | bytes 62939136 | tf_op jit(solution)/shard_map/convert_element_type | solution.py:236
  315.2 4.4 copy-done.2
  319.7 6.1 fusion.99
  325.8 8.0 bitcast_add_fusion.2
  333.9 5.1 pad_maximum_fusion
  344.8 4.5 fusion.88
  349.4 6.4 fusion.68
  355.8 11.6 %bitcast_add_fusion.1 = bf16[2048,6,64]{0,2,1:T(8,128)(2,1)S(1)} fusion(f32[2048,6,64]{0,2,1:T(8,128)} %fusion.68, bf16[512,6,64]{0,2,1:T(8,128)(2,1)S(1)} %bitcast.137, f32[6,512,2048]{2,1,0:T(8,128)} %get-tuple-element.253, f32[6,512]{1,0:T(8,128)S(1)} %log_add_fusion), kind=kOutput, calls=%fused_computation.109 | convolution fusion | flops 819462144 | bytes 30289920 | tf_op jit(solution)/shard_map/hqk,qhd->khd/dot_general | solution.py:253
  375.9 6.6 bitcast_convert_fusion
  382.5 9.3 fusion.105
  392.5 34.9 %multiply_convert_fusion.3 = (bf16[2048,1536]{1,0:T(8,128)(2,1)}, f32[2048,1536]{1,0:T(8,128)}, f32[2048,1536]{1,0:T(8,128)}) fusion(f32[1536]{0:T(1024)S(1)} %copy-done.64, bf16[2048,768]{1,0:T(8,128)(2,1)} %all-gather.11.cloned.1.call-done, bf16[768,1536]{1,0:T(8,128)(2,1)} %all-gather.13.cloned.1.call-done), kind=kOutput, calls=%fused_computation.25 | convolution fusion | flops 5039456256 | bytes 36968448 | tf_op jit(solution)/shard_map/dot_general | solution.py:192
  427.3 17.0 %convert_reduce_fusion = (f32[1536]{0:T(1024)S(1)}, bf16[2048,1536]{1,0:T(8,128)(2,1)S(1)}) fusion(f32[2048,1536]{1,0:T(8,128)} %get-tuple-element.212, bf16[2048,768]{1,0:T(8,128)(2,1)} %all-gather.17.cloned.1.call-done, bf16[768,1536]{1,0:T(8,128)(2,1)} %all-gather.15.cloned.1.call-done, f32[2048,1536]{1,0:T(8,128)} %get-tuple-element.245, ...), kind=kOutput, calls=%fused_computation.19 | convolution fusion | flops 4885314048 | bytes 36974592 | tf_op jit(solution)/shard_map/dot_general | solution.py:209
  446.9 6.4 convolution_convert_fusion
  454.0 7.7 fusion.104
  461.8 4.1 fusion.103
  466.0 11.1 %fusion.106 = bf16[6,64,512]{2,1,0:T(8,128)(2,1)S(1)} fusion(f32[6,512,2048]{2,1,0:T(8,128)} %get-tuple-element.253, f32[6,512]{1,0:T(8,128)S(1)} %copy-done.60, f32[6,512]{1,0:T(8,128)S(1)} %copy-done.58, bf16[2048,6,192]{0,2,1:T(8,128)(2,1)} %copy-done.9), kind=kOutput, calls=%fused_computation.174 | convolution fusion | flops 824377344 | bytes 27156480 | tf_op jit(solution)/shard_map/hqk,khd->qhd/dot_general | solution.py:179
  477.1 7.3 fusion.155
  484.5 4.6 fusion.22
  489.1 3.3 fusion.80
  494.4 10.0 fusion.33
  504.5 9.8 fusion.156
  514.4 9.7 convolution_bitcast_fusion
  524.1 6.2 copy.69
  531.7 3.9 fusion.45
  535.6 3.3 fusion.50
  539.0 6.5 convert_reduce_fusion.5
  545.5 37.6 %all-reduce.25 = (f32[768]{0:T(1024)S(1)}, f32[768]{0:T(1024)S(1)}, f32[768]{0:T(1024)S(1)}, f32[768]{0:T(1024)S(1)}, f32[2304]{0:T(1024)S(1)}, /*index=5*/f32[768]{0:T(1024)S(1)}, f32[3072]{0:T(1024)S(1)}) all-reduce(f32[768]{0:T(1024)S(1)} %get-tuple-element.187, ...), channel_id=5, replica_groups=mesh['dp'=16,'tensor'=2] {'dp','tensor'}, use_global_device_ids=true, to_apply=%region_25.26.clone | all-reduce | flops 9216 | bytes 73728
  586.7 45.2 %reduce-scatter.18.cloned.1.call-done = f32[48,6,64]{2,0,1:T(8,128)} async-done(((f32[768,6,64]{2,0,1:T(8,128)}), f32[48,6,64]{2,0,1:T(8,128)}) %reduce-scatter.18.cloned.1.call-update) | async-done | bytes 73744 | tf_op jit(solution)/shard_map/reduce_scatter | solution.py:314
  631.9 141.2 %reduce-scatter.16.cloned.1.call-done = f32[48,6,192]{2,0,1:T(8,128)} async-done(((f32[768,6,192]{2,0,1:T(8,128)}), f32[48,6,192]{2,0,1:T(8,128)}) %reduce-scatter.16.cloned.1.call-update) | async-done | bytes 221200 | tf_op jit(solution)/shard_map/reduce_scatter | solution.py:313
  773.2 142.5 %reduce-scatter.20.cloned.1.call-done = f32[48,1536]{1,0:T(8,128)} async-done(((f32[768,1536]{1,0:T(8,128)}), f32[48,1536]{1,0:T(8,128)}) %reduce-scatter.20.cloned.1.call-update) | async-done | bytes 294928 | tf_op jit(solution)/shard_map/reduce_scatter | solution.py:315
  915.7 141.4 %reduce-scatter.22.cloned.1.call-done = f32[48,1536]{1,0:T(8,128)} async-done(((f32[768,1536]{1,0:T(8,128)}), f32[48,1536]{1,0:T(8,128)}) %reduce-scatter.22.cloned.1.call-update) | async-done | bytes 294928
  (298 shorter events, 73.3 us)
Async XLA Ops:
  7.2 92.2 %copy-start.3 = (bf16[1024,768]{1,0:T(8,128)(2,1)S(1)}, bf16[1024,768]{1,0:T(8,128)(2,1)}, u32[]{:S(2)}) copy-start(bf16[1024,768]{1,0:T(8,128)(2,1)} %param.35) | copy-start | bytes 4718596
  7.2 149.9 %all-gather.17.cloned.1.call-start = ((), (), s32[]{:S(2)}) async-start(), calls=%async_computation.13 | async-start | bytes 4718592 | tf_op jit(solution)/shard_map/all_gather | solution.py:208
  7.9 153.8 %all-gather.9.cloned.1.call-start = ((), (), s32[]{:S(2)}) async-start(), calls=%async_computation.8 | async-start | bytes 2506752 | tf_op jit(solution)/shard_map/all_gather | solution.py:68
  8.7 156.3 %all-gather.7.cloned.1.call-start = ((), (), s32[]{:S(2)}) async-start(), calls=%async_computation.7 | async-start | bytes 4718592 | tf_op jit(solution)/shard_map/all_gather | solution.py:122
  97.7 5.5 copy-start.46
  97.7 5.5 copy-start.48
  103.2 288.6 %all-gather.11.cloned.1.call-start = ((), (), s32[]{:S(2)}) async-start(), calls=%async_computation.9 | async-start | bytes 4718592 | tf_op jit(solution)/shard_map/all_gather | solution.py:123
  103.8 288.1 %all-gather.13.cloned.1.call-start = ((), (), s32[]{:S(2)}) async-start(), calls=%async_computation.10 | async-start | bytes 2506752 | tf_op jit(solution)/shard_map/all_gather | solution.py:70
  104.4 322.9 %all-gather.15.cloned.1.call-start = ((), (), s32[]{:S(2)}) async-start(), calls=%async_computation.11 | async-start | bytes 2506752 | tf_op jit(solution)/shard_map/all_gather | solution.py:71
  105.0 426.6 %reduce-scatter.14.cloned.1.call-start = ((), (), s32[]{:S(2)}) async-start(), calls=%async_computation.15 | async-start | bytes 4718592 | tf_op jit(solution)/shard_map/reduce_scatter | solution.py:279
  105.9 66.1 %copy-start.33 = (f32[2048,16]{0,1:T(8,128)}, f32[2048,16]{0,1:T(8,128)S(1)}, u32[]{:S(2)}) copy-start(f32[2048,16]{0,1:T(8,128)S(1)} %get-tuple-element.237) | copy-start | bytes 393220
  105.9 66.1 %copy-start.35 = (f32[2048,16]{0,1:T(8,128)}, f32[2048,16]{0,1:T(8,128)S(1)}, u32[]{:S(2)}) copy-start(f32[2048,16]{0,1:T(8,128)S(1)} %get-tuple-element.238) | copy-start | bytes 393220
  150.0 10.5 copy-start.18
  171.7 22.8 %copy-start.9 = (bf16[2048,6,192]{0,2,1:T(8,128)(2,1)}, bf16[2048,6,192]{0,2,1:T(8,128)(2,1)S(1)}, u32[]{:S(2)}) copy-start(bf16[2048,6,192]{0,2,1:T(8,128)(2,1)S(1)} %convert.33) | copy-start | bytes 14155780
  171.9 88.8 %copy-start.5 = (bf16[2048,6,48]{0,2,1:T(8,128)(2,1)}, bf16[2048,6,48]{0,2,1:T(8,128)(2,1)S(1)}, u32[]{:S(2)}) copy-start(bf16[2048,6,48]{0,2,1:T(8,128)(2,1)S(1)} %get-tuple-element.219) | copy-start | bytes 3538948
  174.8 7.2 copy-start.1
  191.9 8.8 copy-start
  194.5 6.1 copy-start.55
  211.7 8.4 copy-start.6
  260.7 10.8 %copy-start.8 = (f32[2048,6,64]{0,2,1:T(8,128)}, f32[2048,6,64]{0,2,1:T(8,128)S(1)}, u32[]{:S(2)}) copy-start(f32[2048,6,64]{0,2,1:T(8,128)S(1)} %fusion.61) | copy-start | bytes 9437188
  271.5 10.5 copy-start.57
  271.5 10.5 copy-start.21
  282.0 16.2 %copy-start.59 = (f32[6,512]{1,0:T(8,128)}, f32[6,512]{1,0:T(8,128)S(1)}, u32[]{:S(2)}) copy-start(f32[6,512]{1,0:T(8,128)S(1)} %fusion) | copy-start | bytes 36868
  325.8 8.1 copy-start.14
  325.8 8.1 copy-start.15
  325.8 8.1 copy-start.16
  325.8 18.1 %slice-start = ((s8[12582912]{0:T(1024)(128)(4,1)}), s8[4194304]{0:T(1024)(128)(4,1)S(1)}, s32[]{:S(2)}) async-start(s8[12582912]{0:T(1024)(128)(4,1)} %bitcast.129), calls=%async_computation.20 | async-start | bytes 8388608
  325.8 18.1 %slice-start.1 = ((s8[12582912]{0:T(1024)(128)(4,1)}), s8[4194304]{0:T(1024)(128)(4,1)S(1)}, s32[]{:S(2)}) async-start(s8[12582912]{0:T(1024)(128)(4,1)} %bitcast.129), calls=%async_computation.21 | async-start | bytes 8388608
  325.8 23.6 %slice-start.3 = ((s8[18874368]{0:T(1024)(128)(4,1)}), s8[4194304]{0:T(1024)(128)(4,1)S(1)}, s32[]{:S(2)}) async-start(s8[18874368]{0:T(1024)(128)(4,1)} %bitcast.131), calls=%async_computation.23 | async-start | bytes 8388608
  325.8 23.6 %slice-start.4 = ((s8[18874368]{0:T(1024)(128)(4,1)}), s8[4194304]{0:T(1024)(128)(4,1)S(1)}, s32[]{:S(2)}) async-start(s8[18874368]{0:T(1024)(128)(4,1)} %bitcast.131), calls=%async_computation.24 | async-start | bytes 8388608
  333.9 15.5 %slice-start.5 = ((s8[18874368]{0:T(1024)(128)(4,1)}), s8[4194304]{0:T(1024)(128)(4,1)S(1)}, s32[]{:S(2)}) async-start(s8[18874368]{0:T(1024)(128)(4,1)} %bitcast.131), calls=%async_computation.25 | async-start | bytes 8388608
  340.7 8.7 slice-start.6
  349.4 6.4 copy-start.22
  355.8 11.6 %copy-start.28 = (f32[2048,6,16]{0,2,1:T(8,128)S(1)}, f32[2048,6,16]{0,2,1:T(8,128)}, u32[]{:S(2)}) copy-start(f32[2048,6,16]{0,2,1:T(8,128)} %get-tuple-element.209) | copy-start | bytes 2359300
  391.8 139.8 %reduce-scatter.12.cloned.1.call-start = ((), (), s32[]{:S(2)}) async-start(), calls=%async_computation.14 | async-start | bytes 4718592 | tf_op jit(solution)/shard_map/reduce_scatter | solution.py:282
  427.3 19.6 %copy-start.68 = (bf16[768,1536]{1,0:T(8,128)(2,1)S(1)}, bf16[768,1536]{1,0:T(8,128)(2,1)}, u32[]{:S(2)}) copy-start(bf16[768,1536]{1,0:T(8,128)(2,1)} %all-gather.13.cloned.1.call-done) | copy-start | bytes 7077892
  453.3 8.4 copy-start.43
  453.4 8.4 copy-start.54
  453.4 85.6 %reduce-scatter.10.cloned.1.call-start = ((), (), s32[]{:S(2)}) async-start(), calls=%async_computation.12 | async-start | bytes 4718592 | tf_op jit(solution)/shard_map/reduce_scatter | solution.py:196
  466.0 11.1 %copy-start.67 = (bf16[768,1536]{1,0:T(8,128)(2,1)S(1)}, bf16[768,1536]{1,0:T(8,128)(2,1)}, u32[]{:S(2)}) copy-start(bf16[768,1536]{1,0:T(8,128)(2,1)} %all-gather.15.cloned.1.call-done) | copy-start | bytes 7077892
  477.1 7.3 copy-start.19
  477.1 7.3 copy-start.70
  489.1 142.9 %reduce-scatter.18.cloned.1.call-start = ((), (), s32[]{:S(2)}) async-start(), calls=%async_computation.17 | async-start | bytes 2506752 | tf_op jit(solution)/shard_map/reduce_scatter | solution.py:314
  494.3 278.8 %reduce-scatter.16.cloned.1.call-start = ((), (), s32[]{:S(2)}) async-start(), calls=%async_computation.16 | async-start | bytes 5013504 | tf_op jit(solution)/shard_map/reduce_scatter | solution.py:313
  504.4 411.2 %reduce-scatter.20.cloned.1.call-start = ((), (), s32[]{:S(2)}) async-start(), calls=%async_computation.18 | async-start | bytes 5013504 | tf_op jit(solution)/shard_map/reduce_scatter | solution.py:315
  514.3 542.7 %reduce-scatter.22.cloned.1.call-start = ((), (), s32[]{:S(2)}) async-start(), calls=%async_computation.19 | async-start | bytes 5013504
  530.3 5.3 copy-start.52
  583.8 473.7 %copy-start.71 = (f32[24]{0:T(128)}, f32[24]{0:T(128)S(1)}, u32[]{:S(2)}) copy-start(f32[24]{0:T(128)S(1)} %dynamic-slice.72) | copy-start | bytes 292
  (48 other events, 122.7 us)
Sparse Core Ops, SparseCore 0:
  9.6 14.8 all-gather.16
  27.1 64.0 all-gather.8
  103.4 7.9 all-gather.6
  112.8 13.2 all-gather.10
  128.8 63.9 all-gather.12
  195.5 61.1 all-gather.14
  391.9 8.4 reduce-scatter.13
  453.5 8.4 reduce-scatter.11
  489.2 7.8 reduce-scatter.9
  503.2 128.6 reduce-scatter.17
  637.7 135.4 reduce-scatter.15
  779.6 136.0 reduce-scatter.19
  921.4 135.5 reduce-scatter.21
where the time goes:
time: 1070 us; the launch traced here: 1060 us
  waiting for transfers between devices  473 us (44%)
  matrix products  264 us (25%)
  blocking collectives  161 us (15%)
  other arithmetic  102 us (10%)
  local copies, waits for them, and re-layouts  46.6 us (4%)
  between operations  17.3 us (2%)
    unnamed x14, waiting for transfers between devices  144 us
    reduce_scatter x1, waiting for transfers between devices, body(): lax.psum_scatter(grad_fc, 'dp', scatter_dimension=0, tiled=True)  142 us
    reduce_scatter x1, waiting for transfers between devices, body(): lax.psum_scatter(grad_qkv, 'dp', scatter_dimension=0, tiled=True)  141 us
    unnamed x2, blocking collectives  117 us
    reduce_scatter x1, waiting for transfers between devices, body(): lax.psum_scatter(grad_dense, 'dp', scatter_dimension=0, tiled=True)  45.2 us
    all_gather x1, blocking collectives, body(): lax.all_gather(dense_weight, 'dp', axis=0, tiled=True)  44.1 us
    convert_element_type x4, other arithmetic, body(): grad_scores = (probs * (grad_probs - row_delta)).astype(jnp.bfloat16)  40.9 us
    dot_general x4, matrix products, body(): jnp.einsum('qhd,khd->hqk', heads_blk, value_low[:end_row], preferred_elem...  39.2 us
  transfers between devices with their start and end apart: 13, of which 4 were waited for; matrix products, arithmetic and copies ran while one was open for 37% of the time, Pallas kernels for 0%

commit v1 on v0

--- a/solution.py
+++ b/solution.py
@@ -2,6 +2,23 @@
 import jax.numpy as jnp
 from jax import lax
 from jax.sharding import PartitionSpec as P
+
+
+def joined_along(blocks, dim):
+    lengths = list(blocks.shape[1:])
+    lengths[dim] *= blocks.shape[0]
+    return jnp.moveaxis(blocks, 0, dim).reshape(lengths)
+
+
+def collect(array, axis, dim):
+    size = lax.axis_size(axis)
+    forward = [(i, (i + 1) % size) for i in range(size)]
+    parts = [array]
+    while len(parts) < size:
+        parts.append(lax.ppermute(parts[-1], axis, forward))
+    index = lax.axis_index(axis)
+    parts = jnp.stack(parts)[(index - jnp.arange(size)) % size]
+    return joined_along(parts, dim)
 
 
 def layout(lengths, group_rows):
@@ -66,7 +83,7 @@
     group_rows = local_rows * tensor_count
     gathered = (
         lax.all_gather(qkv_weight, "dp", axis=0, tiled=True),
-        lax.all_gather(dense_weight, "dp", axis=0, tiled=True),
+        collect(dense_weight, "dp", 0),
         lax.all_gather(fc_weight, "dp", axis=0, tiled=True),
         lax.all_gather(proj_weight, "dp", axis=0, tiled=True),
         lax.all_gather(attn_gain, "dp", axis=0, tiled=True),

time: 1070 us -> 1210 us (1.13)
  waiting for transfers between devices: 473 us -> 593 us
    ppermute x0 -> x15, waiting for transfers between devices: none -> 120 us  [collect(): parts.append(lax.ppermute(parts[-1], axis, forward))]
    unnamed x188 -> x201, local copies, waits for them, and re-layouts: 34.7 us -> 35 us
  transfers between devices with their start and end apart: 13 -> 28, of which waited for: 4 -> 18; matrix products, arithmetic and copies ran while one was open for 37% -> 33% of each run, Pallas kernels for 0% -> 0%
where the time goes in v1:
time: 1210 us; the launch traced here: 1200 us
  waiting for transfers between devices  593 us (49%)
  matrix products  264 us (22%)
  blocking collectives  165 us (14%)
  other arithmetic  101 us (8%)
  local copies, waits for them, and re-layouts  49.9 us (4%)
  between operations  17.4 us (1%)
    unnamed x14, waiting for transfers between devices  145 us
    reduce_scatter x1, waiting for transfers between devices, body(): lax.psum_scatter(grad_fc, 'dp', scatter_dimension=0, tiled=True)  142 us
    reduce_scatter x1, waiting for transfers between devices, body(): lax.psum_scatter(grad_qkv, 'dp', scatter_dimension=0, tiled=True)  142 us
    ppermute x15, waiting for transfers between devices, collect(): parts.append(lax.ppermute(parts[-1], axis, forward))  120 us
    unnamed x2, blocking collectives  117 us
    all_gather x1, blocking collectives, body(): lax.all_gather(dense_weight, 'dp', axis=0, tiled=True)  48.5 us
    reduce_scatter x1, waiting for transfers between devices, body(): lax.psum_scatter(grad_dense, 'dp', scatter_dimension=0, tiled=True)  44.1 us
    convert_element_type x4, other arithmetic, body(): grad_scores = (probs * (grad_probs - row_delta)).astype(jnp.bfloat16)  40.6 us
  transfers between devices with their start and end apart: 28, of which 18 were waited for; matrix products, arithmetic and copies ran while one was open for 33% of the time, Pallas kernels for 0%

profile of v1, /device:TPU:0, one launch (start us, length us, event | category | flops | bytes accessed | tf_op | source)
XLA Modules:
  0.0 1201.7 jit_solution(13932656510108510592)
XLA Ops:
  18.7 79.1 %all-reduce.26 = (bf16[768]{0:T(1024)(128)(2,1)S(1)}, bf16[768]{0:T(1024)(128)(2,1)S(1)}, bf16[3072]{0:T(1024)(128)(2,1)S(1)}, bf16[768]{0:T(1024)(128)(2,1)S(1)...) all-reduce(bf16[768]{0:T(1024)(128)(2,1)S(1)} %dynamic-update-slice, ...), channel_id=1, replica_groups=mesh['dp'=16,'tensor'=2] {'dp'}, use_global_device_ids=true, to_apply=%add.14 | all-reduce | flops 9984 | bytes 39936
  105.5 48.5 %all_gather.62 = bf16[768,6,64]{2,0,1:T(8,128)(2,1)S(1)} all-gather(bf16[48,6,64]{2,0,1:T(8,128)(2,1)S(1)} %copy-done.40), channel_id=1, replica_groups=mesh['dp'=16,'tensor'=2] {'dp'}, dimensions={0}, use_global_device_ids=true | all-gather | bytes 626688 | tf_op jit(solution)/shard_map/all_gather | solution.py:221
  162.4 9.5 collective-permute-done.1
  172.0 8.1 collective-permute-done.2
  180.1 9.0 collective-permute-done.3
  189.1 9.5 collective-permute-done.4
  198.6 7.9 collective-permute-done.5
  206.5 8.9 collective-permute-done.6
  215.4 8.5 collective-permute-done.7
  223.9 9.5 collective-permute-done.8
  233.5 7.9 collective-permute-done.9
  241.4 8.1 collective-permute-done.10
  249.5 9.1 collective-permute-done.11
  258.6 7.9 collective-permute-done.12
  266.6 7.9 collective-permute-done.13
  274.5 10.1 collective-permute-start.14
  284.7 7.9 collective-permute-done.14
  338.8 6.2 multiply_convert_fusion.2
  349.7 8.4 fusion.140
  358.1 9.0 fusion.2
  367.1 12.8 %multiply_reduce_fusion.1 = (f32[6,512]{1,0:T(8,128)S(1)}, f32[6,512,1536]{2,1,0:T(8,128)}) fusion(f32[6,512,1536]{2,1,0:T(8,128)} %get-tuple-element.251, f32[6,512]{1,0:T(8,128)S(1)} %log_add_fusion.1, bf16[512,6,64]{0,2,1:T(8,128)(2,1)} %bitcast.168, bf16[2048,6,192]{0,2,1:T(8,128)(2,1)} %copy-done.9), kind=kOutput, calls=%fused_computation.11 | convolution fusion | flops 618132480 | bytes 39346176 | tf_op jit(solution)/shard_map/qhd,khd->hqk/dot_general | solution.py:249
  379.9 12.9 %multiply_convert_fusion.1 = bf16[6,512,1536]{2,1,0:T(8,128)(2,1)S(1)} fusion(f32[6,512,1536]{2,1,0:T(8,128)} %get-tuple-element.257, f32[6,512,1536]{2,1,0:T(8,128)} %get-tuple-element.251, f32[6,512]{1,0:T(8,128)S(1)} %get-tuple-element.256, f32[6,512]{1,0:T(8,128)S(1)} %log_add_fusion.1), kind=kLoop, calls=%fused_computation.10 | loop fusion | flops 18874368 | bytes 47210496 | tf_op jit(solution)/shard_map/convert_element_type | solution.py:253
  398.6 10.7 fusion.141
  409.3 10.5 fusion
  419.8 16.1 %multiply_reduce_fusion = (f32[6,512]{1,0:T(8,128)S(1)}, f32[6,512,2048]{2,1,0:T(8,128)}) fusion(f32[6,512,2048]{2,1,0:T(8,128)} %get-tuple-element.253, f32[6,512]{1,0:T(8,128)S(1)} %log_add_fusion, bf16[512,6,64]{0,2,1:T(8,128)(2,1)S(1)} %bitcast.166, bf16[2048,6,192]{0,2,1:T(8,128)(2,1)} %copy-done.9), kind=kOutput, calls=%fused_computation.2 | convolution fusion | flops 824177664 | bytes 52322304 | tf_op jit(solution)/shard_map/qhd,khd->hqk/dot_general | solution.py:249
  435.9 16.9 %multiply_convert_fusion = bf16[6,512,2048]{2,1,0:T(8,128)(2,1)S(1)} fusion(f32[6,512,2048]{2,1,0:T(8,128)} %get-tuple-element.255, f32[6,512,2048]{2,1,0:T(8,128)} %get-tuple-element.253, f32[6,512]{1,0:T(8,128)S(1)} %get-tuple-element.254, f32[6,512]{1,0:T(8,128)S(1)} %log_add_fusion), kind=kLoop, calls=%fused_computation.1 | loop fusion | flops 25165824 | bytes 62939136 | tf_op jit(solution)/shard_map/convert_element_type | solution.py:253
  457.3 6.1 fusion.83
  463.5 8.0 bitcast_add_fusion.1
  487.1 6.4 fusion.67
  493.5 11.6 bitcast_add_fusion
  513.6 6.6 bitcast_convert_fusion
  520.1 9.3 fusion.89
  530.1 35.6 %multiply_convert_fusion.3 = (bf16[2048,1536]{1,0:T(8,128)(2,1)}, f32[2048,1536]{1,0:T(8,128)}, f32[2048,1536]{1,0:T(8,128)}) fusion(f32[1536]{0:T(1024)S(1)} %copy-done.64, bf16[2048,768]{1,0:T(8,128)(2,1)} %all-gather.11.cloned.1.call-done, bf16[768,1536]{1,0:T(8,128)(2,1)} %all-gather.13.cloned.1.call-done), kind=kOutput, calls=%fused_computation.26 | convolution fusion | flops 5039456256 | bytes 36968448 | tf_op jit(solution)/shard_map/dot_general | solution.py:209
  565.8 17.0 %convert_reduce_fusion = (f32[1536]{0:T(1024)S(1)}, bf16[2048,1536]{1,0:T(8,128)(2,1)S(1)}) fusion(f32[2048,1536]{1,0:T(8,128)} %get-tuple-element.212, bf16[2048,768]{1,0:T(8,128)(2,1)} %all-gather.17.cloned.1.call-done, bf16[768,1536]{1,0:T(8,128)(2,1)} %all-gather.15.cloned.1.call-done, f32[2048,1536]{1,0:T(8,128)} %get-tuple-element.245, ...), kind=kOutput, calls=%fused_computation.20 | convolution fusion | flops 4885314048 | bytes 36974592 | tf_op jit(solution)/shard_map/dot_general | solution.py:226
  585.4 6.4 convolution_convert_fusion
  592.5 8.0 fusion.88
  604.7 11.1 fusion.90
  615.9 7.3 fusion.142
  632.3 9.8 fusion.32
  642.2 9.9 fusion.143
  652.2 9.7 convolution_bitcast_fusion
  661.9 6.1 copy.72
  676.8 6.5 convert_reduce_fusion.5
  683.3 37.7 %all-reduce.25 = (f32[768]{0:T(1024)S(1)}, f32[768]{0:T(1024)S(1)}, f32[768]{0:T(1024)S(1)}, f32[768]{0:T(1024)S(1)}, f32[2304]{0:T(1024)S(1)}, /*index=5*/f32[768]{0:T(1024)S(1)}, f32[3072]{0:T(1024)S(1)}) all-reduce(f32[768]{0:T(1024)S(1)} %get-tuple-element.187, ...), channel_id=5, replica_groups=mesh['dp'=16,'tensor'=2] {'dp','tensor'}, use_global_device_ids=true, to_apply=%region_25.26.clone | all-reduce | flops 9216 | bytes 73728
  724.6 44.1 %reduce-scatter.18.cloned.1.call-done = f32[48,6,64]{2,0,1:T(8,128)} async-done(((f32[768,6,64]{2,0,1:T(8,128)}), f32[48,6,64]{2,0,1:T(8,128)}) %reduce-scatter.18.cloned.1.call-update) | async-done | bytes 73744 | tf_op jit(solution)/shard_map/reduce_scatter | solution.py:331
  768.7 141.9 %reduce-scatter.16.cloned.1.call-done = f32[48,6,192]{2,0,1:T(8,128)} async-done(((f32[768,6,192]{2,0,1:T(8,128)}), f32[48,6,192]{2,0,1:T(8,128)}) %reduce-scatter.16.cloned.1.call-update) | async-done | bytes 221200 | tf_op jit(solution)/shard_map/reduce_scatter | solution.py:330
  910.6 142.3 %reduce-scatter.20.cloned.1.call-done = f32[48,1536]{1,0:T(8,128)} async-done(((f32[768,1536]{1,0:T(8,128)}), f32[48,1536]{1,0:T(8,128)}) %reduce-scatter.20.cloned.1.call-update) | async-done | bytes 294928 | tf_op jit(solution)/shard_map/reduce_scatter | solution.py:332
  1052.9 141.6 %reduce-scatter.22.cloned.1.call-done = f32[48,1536]{1,0:T(8,128)} async-done(((f32[768,1536]{1,0:T(8,128)}), f32[48,1536]{1,0:T(8,128)}) %reduce-scatter.22.cloned.1.call-update) | async-done | bytes 294928
  (347 shorter events, 140.4 us)
Async XLA Ops:
  7.2 92.3 %copy-start.3 = (bf16[1024,768]{1,0:T(8,128)(2,1)S(1)}, bf16[1024,768]{1,0:T(8,128)(2,1)}, u32[]{:S(2)}) copy-start(bf16[1024,768]{1,0:T(8,128)(2,1)} %param.35) | copy-start | bytes 4718596
  7.2 288.3 %all-gather.17.cloned.1.call-start = ((), (), s32[]{:S(2)}) async-start(), calls=%async_computation.13 | async-start | bytes 4718592 | tf_op jit(solution)/shard_map/all_gather | solution.py:225
  7.9 292.2 %all-gather.9.cloned.1.call-start = ((), (), s32[]{:S(2)}) async-start(), calls=%async_computation.8 | async-start | bytes 2506752 | tf_op jit(solution)/shard_map/all_gather | solution.py:85
  8.7 294.3 %all-gather.7.cloned.1.call-start = ((), (), s32[]{:S(2)}) async-start(), calls=%async_computation.7 | async-start | bytes 4718592 | tf_op jit(solution)/shard_map/all_gather | solution.py:139
  103.3 426.2 %all-gather.11.cloned.1.call-start = ((), (), s32[]{:S(2)}) async-start(), calls=%async_computation.9 | async-start | bytes 4718592 | tf_op jit(solution)/shard_map/all_gather | solution.py:140
  103.9 425.6 %all-gather.13.cloned.1.call-start = ((), (), s32[]{:S(2)}) async-start(), calls=%async_computation.10 | async-start | bytes 2506752 | tf_op jit(solution)/shard_map/all_gather | solution.py:87
  104.5 461.3 %all-gather.15.cloned.1.call-start = ((), (), s32[]{:S(2)}) async-start(), calls=%async_computation.11 | async-start | bytes 2506752 | tf_op jit(solution)/shard_map/all_gather | solution.py:88
  104.6 57.8 %collective-permute-start = (bf16[48,6,64]{2,0,1:T(8,128)(2,1)S(1)}, bf16[48,6,64]{2,0,1:T(8,128)(2,1)S(1)}, u32[]{:S(2)}, u32[]{:S(2)}) collective-permute-start(bf16[48,6,64]{2,0,1:T(8,128)(2,1)S(1)} %copy-done.40), channel_id=1, source_target_pairs={{0,2},{2,4},{4,6},{6,8},{8,10},{10,12},{12,14},{14,16},{16,18},{18... | collective-permute-start | bytes 110600 | tf_op jit(solution)/shard_map/ppermute | solution.py:18
  105.1 564.3 %reduce-scatter.14.cloned.1.call-start = ((), (), s32[]{:S(2)}) async-start(), calls=%async_computation.15 | async-start | bytes 4718592 | tf_op jit(solution)/shard_map/reduce_scatter | solution.py:296
  154.4 155.5 %copy-start.32 = (f32[2048,16]{0,1:T(8,128)}, f32[2048,16]{0,1:T(8,128)S(1)}, u32[]{:S(2)}) copy-start(f32[2048,16]{0,1:T(8,128)S(1)} %get-tuple-element.237) | copy-start | bytes 393220
  154.4 155.5 %copy-start.34 = (f32[2048,16]{0,1:T(8,128)}, f32[2048,16]{0,1:T(8,128)S(1)}, u32[]{:S(2)}) copy-start(f32[2048,16]{0,1:T(8,128)S(1)} %get-tuple-element.238) | copy-start | bytes 393220
  162.4 9.6 collective-permute-start.1
  171.9 8.1 collective-permute-start.2
  180.1 9.0 collective-permute-start.3
  189.1 9.5 collective-permute-start.4
  198.6 7.9 collective-permute-start.5
  206.5 8.9 collective-permute-start.6
  215.4 8.5 collective-permute-start.7
  223.9 9.5 collective-permute-start.8
  233.4 7.9 collective-permute-start.9
  241.4 8.1 collective-permute-start.10
  249.5 9.1 collective-permute-start.11
  258.6 7.9 collective-permute-start.12
  266.6 7.9 collective-permute-start.13
  274.5 18.1 %collective-permute-start.14 = (bf16[48,6,64]{2,0,1:T(8,128)(2,1)S(1)}, bf16[48,6,64]{2,0,1:T(8,128)(2,1)S(1)}, u32[]{:S(2)}, u32[]{:S(2)}) collective-permute-start(bf16[48,6,64]{2,0,1:T(8,128)(2,1)S(1)} %collective-permute-done.13), channel_id=1, source_target_pairs={{0,2},{2,4},{4,6},{6,8},{8,10},{10,12},{12,14},{14,16},{16,18},{18... | collective-permute-start | bytes 110600 | tf_op jit(solution)/shard_map/ppermute | solution.py:18
  309.7 23.0 %copy-start.9 = (bf16[2048,6,192]{0,2,1:T(8,128)(2,1)}, bf16[2048,6,192]{0,2,1:T(8,128)(2,1)S(1)}, u32[]{:S(2)}) copy-start(bf16[2048,6,192]{0,2,1:T(8,128)(2,1)S(1)} %convert.33) | copy-start | bytes 14155780
  309.9 88.7 %copy-start.5 = (bf16[2048,6,48]{0,2,1:T(8,128)(2,1)}, bf16[2048,6,48]{0,2,1:T(8,128)(2,1)S(1)}, u32[]{:S(2)}) copy-start(bf16[2048,6,48]{0,2,1:T(8,128)(2,1)S(1)} %get-tuple-element.219) | copy-start | bytes 3538948
  330.0 8.8 copy-start
  398.5 10.7 copy-start.8
  409.2 10.5 copy-start.57
  409.2 10.5 copy-start.19
  419.7 16.2 %copy-start.59 = (f32[6,512]{1,0:T(8,128)}, f32[6,512]{1,0:T(8,128)S(1)}, u32[]{:S(2)}) copy-start(f32[6,512]{1,0:T(8,128)S(1)} %fusion) | copy-start | bytes 36868
  463.4 18.1 %slice-start = ((s8[12582912]{0:T(1024)(128)(4,1)}), s8[4194304]{0:T(1024)(128)(4,1)S(1)}, s32[]{:S(2)}) async-start(s8[12582912]{0:T(1024)(128)(4,1)} %bitcast.159), calls=%async_computation.20 | async-start | bytes 8388608
  463.4 18.1 %slice-start.1 = ((s8[12582912]{0:T(1024)(128)(4,1)}), s8[4194304]{0:T(1024)(128)(4,1)S(1)}, s32[]{:S(2)}) async-start(s8[12582912]{0:T(1024)(128)(4,1)} %bitcast.159), calls=%async_computation.21 | async-start | bytes 8388608
  463.5 23.6 %slice-start.3 = ((s8[18874368]{0:T(1024)(128)(4,1)}), s8[4194304]{0:T(1024)(128)(4,1)S(1)}, s32[]{:S(2)}) async-start(s8[18874368]{0:T(1024)(128)(4,1)} %bitcast.161), calls=%async_computation.23 | async-start | bytes 8388608
  463.5 23.6 %slice-start.4 = ((s8[18874368]{0:T(1024)(128)(4,1)}), s8[4194304]{0:T(1024)(128)(4,1)S(1)}, s32[]{:S(2)}) async-start(s8[18874368]{0:T(1024)(128)(4,1)} %bitcast.161), calls=%async_computation.24 | async-start | bytes 8388608
  471.6 15.5 %slice-start.5 = ((s8[18874368]{0:T(1024)(128)(4,1)}), s8[4194304]{0:T(1024)(128)(4,1)S(1)}, s32[]{:S(2)}) async-start(s8[18874368]{0:T(1024)(128)(4,1)} %bitcast.161), calls=%async_computation.25 | async-start | bytes 8388608
  478.3 8.7 slice-start.6
  493.5 11.6 copy-start.26
  529.4 140.0 %reduce-scatter.12.cloned.1.call-start = ((), (), s32[]{:S(2)}) async-start(), calls=%async_computation.14 | async-start | bytes 4718592 | tf_op jit(solution)/shard_map/reduce_scatter | solution.py:299
  565.8 19.6 %copy-start.68 = (bf16[768,1536]{1,0:T(8,128)(2,1)S(1)}, bf16[768,1536]{1,0:T(8,128)(2,1)}, u32[]{:S(2)}) copy-start(bf16[768,1536]{1,0:T(8,128)(2,1)} %all-gather.13.cloned.1.call-done) | copy-start | bytes 7077892
  591.8 84.9 %reduce-scatter.10.cloned.1.call-start = ((), (), s32[]{:S(2)}) async-start(), calls=%async_computation.12 | async-start | bytes 4718592 | tf_op jit(solution)/shard_map/reduce_scatter | solution.py:213
  604.7 11.1 copy-start.67
  626.9 141.8 %reduce-scatter.18.cloned.1.call-start = ((), (), s32[]{:S(2)}) async-start(), calls=%async_computation.17 | async-start | bytes 2506752 | tf_op jit(solution)/shard_map/reduce_scatter | solution.py:331
  632.3 278.4 %reduce-scatter.16.cloned.1.call-start = ((), (), s32[]{:S(2)}) async-start(), calls=%async_computation.16 | async-start | bytes 5013504 | tf_op jit(solution)/shard_map/reduce_scatter | solution.py:330
  642.2 410.7 %reduce-scatter.20.cloned.1.call-start = ((), (), s32[]{:S(2)}) async-start(), calls=%async_computation.18 | async-start | bytes 5013504 | tf_op jit(solution)/shard_map/reduce_scatter | solution.py:332
  652.1 542.4 %reduce-scatter.22.cloned.1.call-start = ((), (), s32[]{:S(2)}) async-start(), calls=%async_computation.19 | async-start | bytes 5013504
  721.7 473.3 %copy-start.70 = (f32[24]{0:T(128)}, f32[24]{0:T(128)S(1)}, u32[]{:S(2)}) copy-start(f32[24]{0:T(128)S(1)} %dynamic-slice.72) | copy-start | bytes 292
  (62 other events, 224.7 us)
Sparse Core Ops, SparseCore 0:
  9.6 14.8 all-gather.16
  27.1 64.8 all-gather.8
  103.4 7.9 all-gather.6
  112.9 13.2 all-gather.10
  128.8 66.1 all-gather.12
  197.6 65.1 all-gather.14
  529.6 6.7 reduce-scatter.13
  591.9 6.7 reduce-scatter.11
  627.1 6.7 reduce-scatter.9
  640.0 128.6 reduce-scatter.17
  774.5 136.1 reduce-scatter.15
  917.0 135.8 reduce-scatter.19
  1058.6 135.8 reduce-scatter.21
